TPU v7x, 32 devices: a whole 2x2x4 slice. The times are simulated.
32 devices in a mesh: dp: 2 (over x), ctx: 16 (over z, y, core).
Axes of the slice: x: 2, y: 2, z: 4, core: 2. Of those that a mesh axis runs over, the one named last changes fastest.
Arguments:
- queries: bfloat16 [4096, 1024], P(('dp', 'ctx')), parts along dimension 0, may hold values from -8 to 8
- keys: bfloat16 [4096, 1024], P(('dp', 'ctx')), parts along dimension 0, may hold values from -8 to 8
- values: bfloat16 [4096, 1024], P(('dp', 'ctx')), parts along dimension 0, may hold values from -6 to 6
- grad_out: bfloat16 [4096, 1024], P(('dp', 'ctx')), parts along dimension 0, may hold values from -6 to 6
- rand_blocks: int32 [64, 3], P(('dp', 'ctx')), parts along dimension 0, may hold values from 0 to 1
- global_ids: int32 [4], P('dp'), parts along dimension 0, may hold values from 0 to 31
Outputs:
- attended: bfloat16 [4096, 1024], P(('dp', 'ctx')), parts along dimension 0
- grad_queries: bfloat16 [4096, 1024], P(('dp', 'ctx')), parts along dimension 0
- grad_keys: bfloat16 [4096, 1024], P(('dp', 'ctx')), parts along dimension 0
- grad_values: bfloat16 [4096, 1024], P(('dp', 'ctx')), parts along dimension 0
There are 2 independent parts, one for each index of `dp`. A program takes and returns all parts, laid end to end along the dimension named above; each array names one. Nothing has to cross between parts.
All inputs are finite; a program needn't handle non-finite values.
Results may differ from a plain program's by a relative error of at most 0.02.
Values may be sent and summed in bfloat16 or wider, within the bound.
A program may use at most 128 MiB of HBM per device.

v0:
```python
import jax
import jax.numpy as jnp
from jax import lax
from jax.sharding import PartitionSpec as P

HEADS = 16
HEAD_DIM = 64
BLOCK = 64
RAND = 3
GLOBALS = 2


SCORE_FLOOR = -1e30


def padded_2(array, sides, width):
    for axis, dim in sides:
        size, length = (lax.axis_size(axis), array.shape[dim])
        up = [(i, (i + 1) % size) for i in range(size - 1)]
        down = [(j, i) for i, j in up]
        last = lax.slice_in_dim(array, length - width, length, axis=dim)
        first = lax.slice_in_dim(array, 0, width, axis=dim)
        before = lax.ppermute(last, axis, up)
        after = lax.ppermute(first, axis, down)
        array = jnp.concatenate([before, array, after], axis=dim)
    return array


def from_root(block, axis, source):
    block = jnp.where(lax.axis_index(axis) == source, block, jnp.zeros_like(block))
    return lax.psum(block, axis)


def partner_2(array, axis, distance):
    return lax.ppermute(array, axis, [(i, i ^ 1 << distance) for i in range(lax.axis_size(axis))])


def passed_along(array, axis, by):
    size = lax.axis_size(axis)
    pairs = [(i, i + by) for i in range(size) if 0 <= i + by < size]
    return lax.ppermute(array, axis, pairs)


def attend_blocks(query_blocks, key_blocks, value_blocks, grad_blocks, key_valid):
    scale_factor = HEAD_DIM ** (-0.5)
    scores = (
        jnp.einsum("jqhd,jkhd->jhqk", query_blocks, key_blocks, preferred_element_type=jnp.float32)
        * scale_factor
    )
    scores = jnp.where(key_valid[:, None, None, :], scores, SCORE_FLOOR)
    highest = jnp.max(scores, axis=-1, keepdims=True)
    raw_weights = jnp.exp(scores - highest)
    weight_total = jnp.sum(raw_weights, axis=-1, keepdims=True)
    probs = raw_weights / weight_total
    probs_low = probs.astype(jnp.bfloat16)
    attended = jnp.einsum(
        "jhqk,jkhd->jqhd", probs_low, value_blocks, preferred_element_type=jnp.float32
    )
    grad_probs = jnp.einsum(
        "jqhd,jkhd->jhqk", grad_blocks, value_blocks, preferred_element_type=jnp.float32
    )
    inner = jnp.sum(probs * grad_probs, axis=-1, keepdims=True)
    grad_scores = (scale_factor * probs * (grad_probs - inner)).astype(jnp.bfloat16)
    grad_query = jnp.einsum(
        "jhqk,jkhd->jqhd", grad_scores, key_blocks, preferred_element_type=jnp.float32
    )
    grad_key = jnp.einsum(
        "jhqk,jqhd->jkhd", grad_scores, query_blocks, preferred_element_type=jnp.float32
    )
    grad_value = jnp.einsum(
        "jhqk,jqhd->jkhd", probs_low, grad_blocks, preferred_element_type=jnp.float32
    )
    return (attended, grad_query, grad_key, grad_value, (highest, weight_total, inner))


def local(queries, keys, values, grad_out, rand_blocks, global_ids):
    tok_rows, width = queries.shape
    block_count = tok_rows // BLOCK
    listed = 3 + GLOBALS + RAND
    ctx_count = lax.axis_size("ctx")
    position = lax.axis_index("ctx")
    top_bit = ctx_count.bit_length() - 1
    block_iota = jnp.arange(block_count, dtype=jnp.int32)
    stacked = jnp.stack([keys, values])
    padded = padded_2(stacked, (("ctx", 1),), BLOCK)
    framed = padded.reshape(2, block_count + 2, BLOCK, width)
    window = jnp.concatenate([framed[:, :-2], framed[:, 1:-1], framed[:, 2:]], axis=2)
    owners = global_ids // block_count
    local_ids = global_ids % block_count
    own_pieces = jnp.stack(
        [
            lax.dynamic_slice_in_dim(stacked, local_ids[global_slot] * BLOCK, BLOCK, 1)
            for global_slot in range(GLOBALS)
        ],
        axis=1,
    )
    fetched = jnp.stack(
        [
            from_root(own_pieces[:, global_slot], "ctx", owners[global_slot])
            for global_slot in range(GLOBALS)
        ],
        axis=1,
    )
    global_part = jnp.broadcast_to(
        fetched.reshape(2, 1, GLOBALS * BLOCK, width), (2, block_count, GLOBALS * BLOCK, width)
    )
    pickers = []
    random_parts = []
    for matching in range(RAND):
        spread_bit = top_bit - 1 - matching
        picker = (rand_blocks[:, matching][:, None] == block_iota[None, :]).astype(jnp.bfloat16)
        partner = partner_2(stacked, "ctx", spread_bit).reshape(2, block_count, BLOCK, width)
        chosen = jnp.einsum(
            "jb,sbqd->sjqd", picker, partner, preferred_element_type=jnp.float32
        ).astype(jnp.bfloat16)
        pickers.append(picker)
        random_parts.append(chosen)
    every_key = jnp.concatenate([window, global_part] + random_parts, axis=2)
    key_blocks = every_key[0].reshape(block_count, listed * BLOCK, HEADS, HEAD_DIM)
    value_blocks = every_key[1].reshape(block_count, listed * BLOCK, HEADS, HEAD_DIM)
    global_block = position * block_count + block_iota
    seq_blocks = block_count * ctx_count
    left_ok = global_block > 0
    right_ok = global_block < seq_blocks - 1
    key_valid = jnp.concatenate(
        [
            jnp.broadcast_to(left_ok[:, None], (block_count, BLOCK)),
            jnp.ones((block_count, BLOCK), dtype=bool),
            jnp.broadcast_to(right_ok[:, None], (block_count, BLOCK)),
            jnp.ones((block_count, (GLOBALS + RAND) * BLOCK), dtype=bool),
        ],
        axis=1,
    )
    query_blocks = queries.reshape(block_count, BLOCK, HEADS, HEAD_DIM)
    grad_blocks = grad_out.reshape(block_count, BLOCK, HEADS, HEAD_DIM)
    attended, grad_query, grad_key, grad_value, softmax_stats = attend_blocks(
        query_blocks, key_blocks, value_blocks, grad_blocks, key_valid
    )
    split = jnp.stack([grad_key, grad_value]).reshape(2, block_count, listed, BLOCK, width)
    own_window = (
        jnp.pad(split[:, :, 0], ((0, 0), (0, 2), (0, 0), (0, 0)))
        + jnp.pad(split[:, :, 1], ((0, 0), (1, 1), (0, 0), (0, 0)))
        + jnp.pad(split[:, :, 2], ((0, 0), (2, 0), (0, 0), (0, 0)))
    )
    from_right = passed_along(own_window[:, 0], "ctx", -1)
    from_left = passed_along(own_window[:, -1], "ctx", 1)
    own_total = own_window[:, 1:-1]
    own_total = own_total.at[:, -1].add(from_right)
    own_total = own_total.at[:, 0].add(from_left)
    for matching in range(RAND):
        spread_bit = top_bit - 1 - matching
        terms = split[:, :, 3 + GLOBALS + matching]
        routed = jnp.einsum(
            "jb,sjqd->sbqd",
            pickers[matching].astype(jnp.float32),
            terms,
            precision=lax.Precision.HIGHEST,
        )
        own_total = own_total + partner_2(routed, "ctx", spread_bit)
    attended_out = attended.reshape(tok_rows, width).astype(jnp.bfloat16)
    grad_queries = grad_query.reshape(tok_rows, width).astype(jnp.bfloat16)
    grad_keys = own_total[0].reshape(tok_rows, width).astype(jnp.bfloat16)
    grad_values = own_total[1].reshape(tok_rows, width).astype(jnp.bfloat16)
    return (attended_out, grad_queries, grad_keys, grad_values)


def solution(mesh):
    placed = (
        P(("dp", "ctx"), None),
        P(("dp", "ctx"), None),
        P(("dp", "ctx"), None),
        P(("dp", "ctx"), None),
        P(("dp", "ctx"), None),
        P("dp"),
    )
    return jax.shard_map(
        local,
        mesh=mesh,
        in_specs=placed,
        out_specs=(
            P(("dp", "ctx"), None),
            P(("dp", "ctx"), None),
            P(("dp", "ctx"), None),
            P(("dp", "ctx"), None),
        ),
        check_vma=False,
    )
```

profile of v0, /device:TPU:8, one launch (start us, length us, event | category | flops | bytes accessed | tf_op | source)
XLA Modules:
  0.0 287.4 jit_solution(4324799282225984524)
XLA Ops:
  10.7 2.6 collective-permute-start.2
  17.6 2.2 fusion.34
  21.8 4.5 %collective-permute-start.1 = (bf16[2,64,1024]{2,1,0:T(8,128)(2,1)S(1)}, bf16[2,64,1024]{2,1,0:T(8,128)(2,1)S(1)}, u32[]{:S(2)}, u32[]{:S(2)}) collective-permute-start(bf16[2,64,1024]{2,1,0:T(8,128)(2,1)S(1)} %get-tuple-element.48), channel_id=1, source_target_pairs={{1,0},{2,1},{3,2},{4,3},{5,4},{6,5},{7,6},{8,7},{9,8},{10,9},{11,1... | collective-permute-start | bytes 786440 | tf_op jit(solution)/shard_map/ppermute | solution.py:24
  32.0 8.5 %collective-permute-done = bf16[2,64,1024]{2,1,0:T(8,128)(2,1)S(1)} collective-permute-done((bf16[2,64,1024]{2,1,0:T(8,128)(2,1)S(1)}, bf16[2,64,1024]{2,1,0:T(8,128)(2,1)S(1)}, u32[]{:S(2)}, u32[]{:S(2)}) %collective-permute-start) | collective-permute-done | bytes 262176 | tf_op jit(solution)/shard_map/ppermute | solution.py:23
  41.6 78.3 %all-reduce.6.cloned.1.call-done = (bf16[2,1,64,1024]{3,2,1,0:T(8,128)(2,1)}, bf16[2,1,64,1024]{3,2,0,1:T(8,128)(2,1)}) async-done(((bf16[2,1,64,1024]{3,2,1,0:T(8,128)(2,1)}, bf16[2,1,64,1024]{3,2,0,1:T(8,128)(2,1)}), (bf16[2,1,64,1024]{3,2,1,0:T(8,128)(2,1)}, bf16[2,1,64,1024]{3,2,0,1:T(8,128)(2,1)})) %all-reduce.6.cloned.1.call-update) | async-done | bytes 524304 | tf_op jit(solution)/shard_map/psum | solution.py:31
  124.6 2.6 fusion.15
  127.2 2.3 copy.44
  129.5 2.6 fusion.13
  132.1 2.3 copy.42
  134.4 2.6 fusion.14
  137.0 2.3 copy.43
  139.3 2.2 broadcast_in_dim.25
  141.5 10.3 %concatenate.15 = bf16[2,2,512,1024]{2,3,1,0:T(8,128)(2,1)} concatenate(bf16[2,2,64,1024]{2,3,1,0:T(8,128)(2,1)S(1)} %copy.75, bf16[2,2,64,1024]{2,3,1,0:T(8,128)(2,1)S(1)} %copy.76, bf16[2,2,64,1024]{2,3,1,0:T(8,128)(2,1)S(1)} %copy.77, bf16[2,2,128,1024]{2,3,1,0:T(8,128)(2,1)} %broadcast_in_dim.25, bf16[2,2,64,1024]{2,3,1,0:T(8,128)(2,1)} %copy.42, ...), dimensions={2} | concatenate | bytes 8388608 | tf_op jit(solution)/shard_map/concatenate | solution.py:118
  151.8 4.0 %fusion.51 = (bf16[1,2,512,1024]{2,3,1,0:T(8,128)(2,1)S(1)}, bf16[1,2,512,1024]{2,3,1,0:T(8,128)(2,1)}) fusion(bf16[2,2,512,1024]{2,3,1,0:T(8,128)(2,1)} %concatenate.15), kind=kLoop, calls=%fused_computation.99 | loop fusion | bytes 8388608 | tf_op jit(solution)/shard_map/slice | solution.py:119
  155.8 3.4 %fusion.57 = (f32[2,16,64]{2,1,0:T(8,128)S(1)}, f32[2,16,64,512]{3,2,1,0:T(8,128)}) fusion(pred[2,512]{1,0:T(4,128)(4,1)S(1)} %add_add_fusion, bf16[2,64,16,64]{1,3,2,0:T(8,128)(2,1)S(1)} %copy-done.9, bf16[2,512,16,64]{1,3,2,0:T(8,128)(2,1)S(1)} %bitcast.133), kind=kOutput, calls=%fused_computation.105 | convolution fusion | flops 138412544 | bytes 6562816 | tf_op jit(solution)/shard_map/sub | solution.py:52
  159.2 5.0 %convolution_bitcast_fusion = f32[2,512,16,64]{1,3,2,0:T(8,128)} fusion(bf16[2,64,16,64]{1,3,2,0:T(8,128)(2,1)S(1)} %copy-done.10, f32[2,16,64,512]{3,2,1,0:T(8,128)} %get-tuple-element.57, f32[2,16,64]{2,1,0:T(8,128)S(1)} %get-tuple-element.56), kind=kOutput, calls=%fused_computation.11 | convolution fusion | flops 136314880 | bytes 8658944 | tf_op jit(solution)/shard_map/jhqk,jqhd->jkhd/dot_general | solution.py:70
  166.5 2.6 convolution_bitcast_fusion.1
  169.1 7.1 %reshape.141 = f32[1,2,8,64,1024]{3,2,4,1,0:T(8,128)} reshape(f32[2,512,16,64]{1,3,2,0:T(8,128)} %convolution_bitcast_fusion.1) | data formatting | bytes 8388608 | tf_op jit(solution)/shard_map/stack | solution.py:139
  176.2 8.6 %copy.53 = f32[1,2,8,64,1024]{4,1,3,0,2:T(2,128)} copy(f32[1,2,8,64,1024]{3,2,4,1,0:T(8,128)} %reshape.141) | data formatting | bytes 8388608 | tf_op jit(solution)/shard_map/stack | solution.py:139
  184.8 7.1 %reshape.142 = f32[1,2,8,64,1024]{3,2,4,1,0:T(8,128)} reshape(f32[2,512,16,64]{1,3,2,0:T(8,128)} %convolution_bitcast_fusion) | data formatting | bytes 8388608 | tf_op jit(solution)/shard_map/stack | solution.py:139
  191.9 8.6 %copy.54 = f32[1,2,8,64,1024]{4,1,3,0,2:T(2,128)} copy(f32[1,2,8,64,1024]{3,2,4,1,0:T(8,128)} %reshape.142) | data formatting | bytes 8388608 | tf_op jit(solution)/shard_map/stack | solution.py:139
  200.6 3.6 %fusion.20 = f32[2,64,1024,2]{2,3,1,0:T(2,128)S(1)} fusion(f32[1,2,8,64,1024]{4,1,3,0,2:T(2,128)} %copy.54, f32[1,2,8,64,1024]{4,1,3,0,2:T(2,128)} %copy.53, s32[2]{0:T(128)S(1)} %get-tuple-element.30), kind=kOutput, calls=%fused_computation.43 | convolution fusion | flops 6553604 | bytes 9437192 | tf_op jit(solution)/shard_map/jb,sjqd->sbqd/dot_general | solution.py:153
  204.3 2.3 fusion.19
  206.7 2.3 fusion.21
  215.9 2.1 fusion.52
  218.9 2.2 collective-permute-start.5
  226.8 2.2 copy.46
  229.1 2.1 convert_element_type.71
  231.2 2.0 copy.99
  235.1 3.1 %fusion.12 = bf16[2,64,16,64]{1,3,2,0:T(8,128)(2,1)} fusion(bf16[2,512,16,64]{1,3,2,0:T(8,128)(2,1)} %bitcast.134, bf16[2,16,64,512]{3,2,1,0:T(8,128)(2,1)S(1)} %fusion.3), kind=kOutput, calls=%fused_computation.24 | convolution fusion | flops 134348800 | bytes 4456448 | tf_op jit(solution)/shard_map/jhqk,jkhd->jqhd/dot_general | solution.py:64
  242.4 33.9 %collective-permute-done.6 = f32[2,64,1024]{2,1,0:T(8,128)} collective-permute-done((f32[2,64,1024]{2,1,0:T(8,128)}, f32[2,64,1024]{2,1,0:T(8,128)}, u32[]{:S(2)}, u32[]{:S(2)}) %collective-permute-start.6) | collective-permute-done | bytes 524320 | tf_op jit(solution)/shard_map/ppermute | solution.py:41
  277.5 2.2 add_convert_fusion
  (80 shorter events, 42.4 us)
Async XLA Ops:
  7.2 33.3 %copy-start.6 = (bf16[128,1024]{1,0:T(8,128)(2,1)S(1)}, bf16[128,1024]{1,0:T(8,128)(2,1)}, u32[]{:S(2)}) copy-start(bf16[128,1024]{1,0:T(8,128)(2,1)} %param.12) | copy-start | bytes 786436
  7.2 33.3 %copy-start.5 = (bf16[128,1024]{1,0:T(8,128)(2,1)S(1)}, bf16[128,1024]{1,0:T(8,128)(2,1)}, u32[]{:S(2)}) copy-start(bf16[128,1024]{1,0:T(8,128)(2,1)} %param.11) | copy-start | bytes 786436
  7.2 23.0 %copy-start.11 = (bf16[128,1024]{1,0:T(8,128)(2,1)S(1)}, bf16[128,1024]{1,0:T(8,128)(2,1)}, u32[]{:S(2)}) copy-start(bf16[128,1024]{1,0:T(8,128)(2,1)} %param.13) | copy-start | bytes 786436
  7.2 112.8 %all-reduce.6.cloned.1.call-start = ((), (), s32[]{:S(2)}) async-start(), calls=%async_computation | async-start | bytes 1048576 | tf_op jit(solution)/shard_map/psum | solution.py:31
  9.2 115.3 %collective-permute-start.4 = (bf16[2,128,1024]{2,1,0:T(8,128)(2,1)}, bf16[2,128,1024]{2,1,0:T(8,128)(2,1)}, u32[]{:S(2)}, u32[]{:S(2)}) collective-permute-start(bf16[2,128,1024]{2,1,0:T(8,128)(2,1)} %pad_maximum_fusion.2), channel_id=1, source_target_pairs={{0,2},{1,3},{2,0},{3,1},{4,6},{5,7},{6,4},{7,5},{8,10},{9,11},{10,... | collective-permute-start | bytes 1572872 | tf_op jit(solution)/shard_map/ppermute | solution.py:35
  10.7 118.7 %collective-permute-start.2 = (bf16[2,128,1024]{2,1,0:T(8,128)(2,1)}, bf16[2,128,1024]{2,1,0:T(8,128)(2,1)}, u32[]{:S(2)}, u32[]{:S(2)}) collective-permute-start(bf16[2,128,1024]{2,1,0:T(8,128)(2,1)} %pad_maximum_fusion.2), channel_id=1, source_target_pairs={{0,8},{1,9},{2,10},{3,11},{4,12},{5,13},{6,14},{7,15},{8,0},{9,1},... | collective-permute-start | bytes 1572872 | tf_op jit(solution)/shard_map/ppermute | solution.py:35
  13.3 121.1 %collective-permute-start.3 = (bf16[2,128,1024]{2,1,0:T(8,128)(2,1)}, bf16[2,128,1024]{2,1,0:T(8,128)(2,1)}, u32[]{:S(2)}, u32[]{:S(2)}) collective-permute-start(bf16[2,128,1024]{2,1,0:T(8,128)(2,1)} %pad_maximum_fusion.2), channel_id=1, source_target_pairs={{0,4},{1,5},{2,6},{3,7},{4,0},{5,1},{6,2},{7,3},{8,12},{9,13},{10,... | collective-permute-start | bytes 1572872 | tf_op jit(solution)/shard_map/ppermute | solution.py:35
  19.8 20.7 %collective-permute-start = (bf16[2,64,1024]{2,1,0:T(8,128)(2,1)S(1)}, bf16[2,64,1024]{2,1,0:T(8,128)(2,1)S(1)}, u32[]{:S(2)}, u32[]{:S(2)}) collective-permute-start(bf16[2,64,1024]{2,1,0:T(8,128)(2,1)S(1)} %get-tuple-element.47), channel_id=1, source_target_pairs={{0,1},{1,2},{2,3},{3,4},{4,5},{5,6},{6,7},{7,8},{8,9},{9,10},{10,1... | collective-permute-start | bytes 786440 | tf_op jit(solution)/shard_map/ppermute | solution.py:23
  21.8 18.7 %collective-permute-start.1 = (bf16[2,64,1024]{2,1,0:T(8,128)(2,1)S(1)}, bf16[2,64,1024]{2,1,0:T(8,128)(2,1)S(1)}, u32[]{:S(2)}, u32[]{:S(2)}) collective-permute-start(bf16[2,64,1024]{2,1,0:T(8,128)(2,1)S(1)} %get-tuple-element.48), channel_id=1, source_target_pairs={{1,0},{2,1},{3,2},{4,3},{5,4},{6,5},{7,6},{8,7},{9,8},{10,9},{11,1... | collective-permute-start | bytes 786440 | tf_op jit(solution)/shard_map/ppermute | solution.py:24
  151.8 4.0 %copy-start.9 = (bf16[2,64,16,64]{1,3,2,0:T(8,128)(2,1)S(1)}, bf16[2,64,16,64]{1,3,2,0:T(8,128)(2,1)}, u32[]{:S(2)}) copy-start(bf16[2,64,16,64]{1,3,2,0:T(8,128)(2,1)} %copy.49) | copy-start | bytes 786436
  155.8 8.4 %copy-start.2 = (bf16[1,2,512,1024]{2,3,1,0:T(8,128)(2,1)}, bf16[1,2,512,1024]{2,3,1,0:T(8,128)(2,1)S(1)}, u32[]{:S(2)}) copy-start(bf16[1,2,512,1024]{2,3,1,0:T(8,128)(2,1)S(1)} %get-tuple-element.36) | copy-start | bytes 6291460
  155.8 3.4 %copy-start.10 = (bf16[2,64,16,64]{1,3,2,0:T(8,128)(2,1)S(1)}, bf16[2,64,16,64]{1,3,2,0:T(8,128)(2,1)}, u32[]{:S(2)}) copy-start(bf16[2,64,16,64]{1,3,2,0:T(8,128)(2,1)} %copy.51) | copy-start | bytes 786436
  159.2 5.0 %copy-start.3 = (f32[2,16,64,512]{3,2,1,0:T(8,128)S(1)}, f32[2,16,64,512]{3,2,1,0:T(8,128)}, u32[]{:S(2)}) copy-start(f32[2,16,64,512]{3,2,1,0:T(8,128)} %get-tuple-element.57) | copy-start | bytes 12582916
  159.2 5.0 %copy-start.7 = (bf16[1,2,512,1024]{2,3,1,0:T(8,128)(2,1)S(1)}, bf16[1,2,512,1024]{2,3,1,0:T(8,128)(2,1)}, u32[]{:S(2)}) copy-start(bf16[1,2,512,1024]{2,3,1,0:T(8,128)(2,1)} %get-tuple-element.37) | copy-start | bytes 6291460
  200.6 3.6 %copy-start = (f32[1,2,8,64,1024]{4,1,3,0,2:T(2,128)S(1)}, f32[1,2,8,64,1024]{4,1,3,0,2:T(2,128)}, u32[]{:S(2)}) copy-start(f32[1,2,8,64,1024]{4,1,3,0,2:T(2,128)} %copy.53) | copy-start | bytes 12582916
  200.6 3.8 %copy-start.1 = (f32[1,2,8,64,1024]{4,1,3,0,2:T(2,128)S(1)}, f32[1,2,8,64,1024]{4,1,3,0,2:T(2,128)}, u32[]{:S(2)}) copy-start(f32[1,2,8,64,1024]{4,1,3,0,2:T(2,128)} %copy.54) | copy-start | bytes 12582916
  214.6 10.0 %copy-start.4 = (f32[2,16,64,512]{3,2,1,0:T(8,128)S(1)}, f32[2,16,64,512]{3,2,1,0:T(8,128)}, u32[]{:S(2)}) copy-start(f32[2,16,64,512]{3,2,1,0:T(8,128)} %get-tuple-element.57) | copy-start | bytes 12582916
  214.6 10.0 %copy-start.8 = (bf16[1,2,512,1024]{2,3,1,0:T(8,128)(2,1)S(1)}, bf16[1,2,512,1024]{2,3,1,0:T(8,128)(2,1)}, u32[]{:S(2)}) copy-start(bf16[1,2,512,1024]{2,3,1,0:T(8,128)(2,1)} %get-tuple-element.37) | copy-start | bytes 6291460
  218.9 22.1 %collective-permute-start.5 = (f32[2,64,1024]{2,1,0:T(8,128)}, f32[2,64,1024]{2,1,0:T(8,128)}, u32[]{:S(2)}, u32[]{:S(2)}) collective-permute-start(f32[2,64,1024]{2,1,0:T(8,128)} %bitcast.131), channel_id=1, source_target_pairs={{1,0},{2,1},{3,2},{4,3},{5,4},{6,5},{7,6},{8,7},{9,8},{10,9},{11,1... | collective-permute-start | bytes 1572872 | tf_op jit(solution)/shard_map/ppermute | solution.py:41
  221.1 56.4 %collective-permute-start.9 = (f32[2,2,64,1024]{3,2,0,1:T(8,128)}, f32[2,2,64,1024]{3,2,0,1:T(8,128)}, u32[]{:S(2)}, u32[]{:S(2)}) collective-permute-start(f32[2,2,64,1024]{3,2,0,1:T(8,128)} %bitcast.128), channel_id=1, source_target_pairs={{0,2},{1,3},{2,0},{3,1},{4,6},{5,7},{6,4},{7,5},{8,10},{9,11},{10,... | collective-permute-start | bytes 3145736 | tf_op jit(solution)/shard_map/ppermute | solution.py:35
  221.8 55.8 %collective-permute-start.7 = (f32[2,2,64,1024]{3,2,0,1:T(8,128)}, f32[2,2,64,1024]{3,2,0,1:T(8,128)}, u32[]{:S(2)}, u32[]{:S(2)}) collective-permute-start(f32[2,2,64,1024]{3,2,0,1:T(8,128)} %bitcast.130), channel_id=1, source_target_pairs={{0,8},{1,9},{2,10},{3,11},{4,12},{5,13},{6,14},{7,15},{8,0},{9,1},... | collective-permute-start | bytes 3145736 | tf_op jit(solution)/shard_map/ppermute | solution.py:35
  223.1 54.4 %collective-permute-start.8 = (f32[2,2,64,1024]{3,2,0,1:T(8,128)}, f32[2,2,64,1024]{3,2,0,1:T(8,128)}, u32[]{:S(2)}, u32[]{:S(2)}) collective-permute-start(f32[2,2,64,1024]{3,2,0,1:T(8,128)} %bitcast.129), channel_id=1, source_target_pairs={{0,4},{1,5},{2,6},{3,7},{4,0},{5,1},{6,2},{7,3},{8,12},{9,13},{10,... | collective-permute-start | bytes 3145736 | tf_op jit(solution)/shard_map/ppermute | solution.py:35
  233.2 43.2 %collective-permute-start.6 = (f32[2,64,1024]{2,1,0:T(8,128)}, f32[2,64,1024]{2,1,0:T(8,128)}, u32[]{:S(2)}, u32[]{:S(2)}) collective-permute-start(f32[2,64,1024]{2,1,0:T(8,128)} %bitcast.132), channel_id=1, source_target_pairs={{0,1},{1,2},{2,3},{3,4},{4,5},{5,6},{6,7},{7,8},{8,9},{9,10},{10,1... | collective-permute-start | bytes 1572872 | tf_op jit(solution)/shard_map/ppermute | solution.py:41
Sparse Core Ops, SparseCore 0:
  26.5 93.4 all-reduce.5
where the time goes:
time: 289 us; the launch traced here: 287 us
  waiting for transfers between devices  121 us (42%)
  local copies, waits for them, and re-layouts  83.2 us (29%)
  matrix products  33.1 us (11%)
  starting transfers between devices  18.7 us (6%)
  between operations  16.9 us (6%)
  other arithmetic  14.7 us (5%)
    psum x1, waiting for transfers between devices, from_root(): return lax.psum(block, axis)  78.3 us
    ppermute x2, waiting for transfers between devices, passed_along(): return lax.ppermute(array, axis, pairs)  33.9 us
    another operation x4, local copies, waits for them, and re-layouts, local(): jnp.stack([grad_key, grad_value])  31.5 us
    concatenate x1, local copies, waits for them, and re-layouts, local(): every_key = jnp.concatenate([window, global_part] + random_parts, axis=2)  10.3 us
    ppermute x1, waiting for transfers between devices, padded_2(): before = lax.ppermute(last, axis, up)  8.53 us
    dot_general x3, matrix products, local(): jnp.einsum('jb,sjqd->sbqd', pickers[matching].astype(jnp.float32), terms,...  8.28 us
    ppermute x6, starting transfers between devices, partner_2(): lax.ppermute(array, axis, [(i, i ^ 1 << distance) for i in range(lax.axis...  8.1 us
    dot_general x3, matrix products, local(): jnp.einsum('jb,sbqd->sjqd', picker, partner, preferred_element_type=jnp.f...  7.83 us
  transfers between devices with their start and end apart: 11, of which 3 were waited for; matrix products, arithmetic and copies ran while one was open for 14% of the time, Pallas kernels for 0%

commit v1 on v0

v1 whole, which is shorter than its diff:
```python
import functools

import jax
import jax.numpy as jnp
from jax import lax
from jax.experimental import pallas as pl
from jax.experimental.pallas import tpu as pltpu
from jax.sharding import PartitionSpec as P

HEADS = 16
HEAD_DIM = 64
BLOCK = 64
RAND = 3
GLOBALS = 2
SLAB = 2 * BLOCK
PACK = 2 * HEAD_DIM
EXTRA = 16
SCORE_FLOOR = -1e30


def kernel(
    n,
    q_ref,
    k_ref,
    v_ref,
    g_ref,
    rand_ref,
    gid_ref,
    att_ref,
    dq_ref,
    dk_ref,
    dv_ref,
    a_pack,
    b_pack,
    a_all,
    b_all,
    acc,
    o_send,
    o_all,
    d_send,
    d_all,
    sem_as,
    sem_ar,
    sem_bs,
    sem_br,
    sem_os,
    sem_or,
    sem_ds,
    sem_dr,
):
    share = n // HEADS
    me = lax.axis_index("ctx")
    my_head = me // share
    my_turn = me % share

    def send_a(dest, origin):
        return pltpu.make_async_remote_copy(
            src_ref=a_pack.at[dest // share],
            dst_ref=a_all.at[pl.ds(2 * origin, 2)],
            send_sem=sem_as.at[dest],
            recv_sem=sem_ar.at[origin],
            device_id={"ctx": dest},
            device_id_type=pl.DeviceIdType.MESH,
        )

    def send_b(dest, origin):
        return pltpu.make_async_remote_copy(
            src_ref=b_pack.at[dest // share],
            dst_ref=b_all.at[origin],
            send_sem=sem_bs.at[dest],
            recv_sem=sem_br.at[origin],
            device_id={"ctx": dest},
            device_id_type=pl.DeviceIdType.MESH,
        )

    def send_o(dest, head):
        return pltpu.make_async_remote_copy(
            src_ref=o_send.at[dest],
            dst_ref=o_all.at[head],
            send_sem=sem_os.at[dest],
            recv_sem=sem_or.at[head],
            device_id={"ctx": dest},
            device_id_type=pl.DeviceIdType.MESH,
        )

    def send_d(dest, head):
        return pltpu.make_async_remote_copy(
            src_ref=d_send.at[dest],
            dst_ref=d_all.at[head],
            send_sem=sem_ds.at[dest],
            recv_sem=sem_dr.at[head],
            device_id={"ctx": dest},
            device_id_type=pl.DeviceIdType.MESH,
        )

    barrier = pltpu.get_barrier_semaphore()

    def greet(i, carry):
        pl.semaphore_signal(
            barrier,
            inc=1,
            device_id={"ctx": (me + i) % n},
            device_id_type=pl.DeviceIdType.MESH,
        )
        return carry

    lax.fori_loop(1, n, greet, 0)

    for pair in range(HEADS // 2):
        cols = slice(PACK * pair, PACK * (pair + 1))
        kt, vt = k_ref[:, cols], v_ref[:, cols]
        for odd in range(2):
            half = slice(HEAD_DIM * odd, HEAD_DIM * (odd + 1))
            both = jnp.concatenate([kt[:, half], vt[:, half]], axis=1)
            a_pack[2 * pair + odd] = both.reshape(2, BLOCK, PACK)
    pl.semaphore_wait(barrier, n - 1)

    def start_a(i, carry):
        send_a((me + i) % n, me).start()
        return carry

    lax.fori_loop(1, n, start_a, 0)

    lane = lax.broadcasted_iota(jnp.int32, (1, SLAB), 1)
    low = lane < BLOCK
    rows = [
        jnp.where(low, rand_ref[0, r], rand_ref[1, r]).astype(jnp.float32)
        for r in range(RAND)
    ]
    rows.append(jnp.zeros((EXTRA - RAND, SLAB), jnp.float32))
    picks = jnp.concatenate(rows, axis=0).astype(jnp.bfloat16)
    for pair in range(HEADS // 2):
        cols = slice(PACK * pair, PACK * (pair + 1))
        qt, gt = q_ref[:, cols], g_ref[:, cols]
        for odd in range(2):
            half = slice(HEAD_DIM * odd, HEAD_DIM * (odd + 1))
            b_pack[2 * pair + odd, :SLAB] = jnp.concatenate(
                [qt[:, half], gt[:, half]], axis=1
            )
            b_pack[2 * pair + odd, SLAB:] = picks

    def start_b(i, carry):
        send_b((me + i) % n, me).start()
        return carry

    lax.fori_loop(1, n, start_b, 0)

    a_all[pl.ds(2 * me, 2)] = a_pack[my_head]
    b_all[me] = b_pack[my_head]
    acc[...] = jnp.zeros_like(acc)

    def arrive_a(i, carry):
        send_a(me, (me + n - i) % n).wait_recv()
        return carry

    lax.fori_loop(1, n, arrive_a, 0)

    lane_f = jnp.where(low, 0.125, 0.0)
    keep_q = lane_f.astype(jnp.bfloat16)
    keep_g = jnp.where(low, 0.0, 1.0).astype(jnp.bfloat16)
    fixed = [a_all[gid_ref[slot]] for slot in range(GLOBALS)]

    def partner(c, r):
        d = n // 2 ** (r + 1)
        return c + d - 2 * d * ((c // d) % 2)

    def slab(c):
        mixed = b_all[c]
        tokens = mixed[:SLAB]
        both = jnp.concatenate([tokens * keep_q, tokens * keep_g], axis=0)
        before = jnp.maximum(2 * c - 1, 0)
        after = jnp.minimum(2 * c + 2, 2 * n - 1)
        listed = [a_all[before], a_all[2 * c], a_all[2 * c + 1], a_all[after]]
        for r in range(RAND):
            other = partner(c, r)
            listed += [a_all[2 * other], a_all[2 * other + 1]]
        own_rows = len(listed) * BLOCK
        keys = jnp.concatenate(listed + fixed, axis=0)
        prod = lax.dot_general(
            keys, both, (((1,), (1,)), ((), ())), preferred_element_type=jnp.float32
        )
        scores = prod[:, :SLAB]
        grads = prod[:, SLAB:]
        chosen = mixed[SLAB:].astype(jnp.float32)
        segs = [scores[i * BLOCK : (i + 1) * BLOCK] for i in range(len(listed))]
        left_ok = lane + jnp.where(c > 0, 0, SLAB) < BLOCK
        right_ok = lane - jnp.where(c < n - 1, 0, SLAB) >= BLOCK
        segs[0] = jnp.where(left_ok, segs[0], SCORE_FLOOR)
        segs[3] = jnp.where(right_ok, segs[3], SCORE_FLOOR)
        for r in range(RAND):
            pick = chosen[r : r + 1]
            segs[4 + 2 * r] = jnp.where(pick < 0.5, segs[4 + 2 * r], SCORE_FLOOR)
            segs[5 + 2 * r] = jnp.where(pick > 0.5, segs[5 + 2 * r], SCORE_FLOOR)
        scores = jnp.concatenate(segs + [scores[own_rows:]], axis=0)
        highest = jnp.max(scores, axis=0, keepdims=True)
        raw = jnp.exp(scores - highest)
        inverse = 1.0 / jnp.sum(raw, axis=0, keepdims=True)
        inner = jnp.sum(raw * grads, axis=0, keepdims=True) * inverse
        probs = raw * inverse
        grad_scores = probs * (grads - inner)
        packed = jnp.concatenate(
            [grad_scores.astype(jnp.bfloat16), probs.astype(jnp.bfloat16)], axis=1
        )
        terms = jnp.dot(packed[:own_rows], both, preferred_element_type=jnp.float32)
        out = lax.dot_general(
            keys, packed, (((0,), (0,)), ((), ())), preferred_element_type=jnp.float32
        )
        out = jnp.concatenate(
            [out[:HEAD_DIM, :SLAB] * 0.125, out[HEAD_DIM:, SLAB:]], axis=0
        )
        o_send[c] = out.T.astype(jnp.bfloat16)
        places = [before, 2 * c, 2 * c + 1, after]
        for r in range(RAND):
            other = partner(c, r)
            places += [2 * other, 2 * other + 1]
        for i, place in enumerate(places):
            acc[place] += terms[i * BLOCK : (i + 1) * BLOCK]

    def return_o(c):
        if share == 1:
            send_o(c, my_head).start()
        else:

            @pl.when(c % share == my_turn)
            def _():
                send_o(c, my_head).start()

    slab(me)
    o_all[my_head] = o_send[me]

    def step(i, carry):
        c = (me + n - i) % n
        send_b(me, c).wait_recv()
        slab(c)
        return_o(c)
        return carry

    lax.fori_loop(1, n, step, 0)

    def return_d(i, carry):
        c = ((my_head + HEADS - i) % HEADS) * share + my_turn
        d_send[c] = acc[pl.ds(2 * c, 2)].reshape(SLAB, PACK).astype(jnp.bfloat16)
        send_d(c, my_head).start()
        return carry

    lax.fori_loop(1, HEADS, return_d, 0)
    d_all[my_head] = acc[pl.ds(2 * me, 2)].reshape(SLAB, PACK).astype(jnp.bfloat16)

    def arrive_o(i, carry):
        send_o(me, (my_head + i) % HEADS).wait_recv()
        return carry

    lax.fori_loop(1, HEADS, arrive_o, 0)

    def unpack(source, low_ref, high_ref):
        for pair in range(HEADS // 2):
            cols = slice(PACK * pair, PACK * (pair + 1))
            even, odd = source[2 * pair], source[2 * pair + 1]
            low_ref[:, cols] = jnp.concatenate(
                [even[:, :HEAD_DIM], odd[:, :HEAD_DIM]], axis=1
            )
            high_ref[:, cols] = jnp.concatenate(
                [even[:, HEAD_DIM:], odd[:, HEAD_DIM:]], axis=1
            )

    unpack(o_all, dq_ref, att_ref)

    def arrive_d(i, carry):
        send_d(me, (my_head + i) % HEADS).wait_recv()
        return carry

    lax.fori_loop(1, HEADS, arrive_d, 0)
    unpack(d_all, dk_ref, dv_ref)

    def sent_in(i, carry):
        send_a((me + i) % n, me).wait_send()
        send_b((me + i) % n, me).wait_send()
        return carry

    lax.fori_loop(1, n, sent_in, 0)

    def sent_back(i, carry):
        c = ((my_head + HEADS - i) % HEADS) * share + my_turn
        send_o(c, my_head).wait_send()
        send_d(c, my_head).wait_send()
        return carry

    lax.fori_loop(1, HEADS, sent_back, 0)


def local(n, queries, keys, values, grad_out, rand_blocks, global_ids):
    out = jax.ShapeDtypeStruct(queries.shape, jnp.bfloat16)
    vmem = pl.BlockSpec(memory_space=pltpu.VMEM)
    smem = pl.BlockSpec(memory_space=pltpu.SMEM)
    dma = pltpu.SemaphoreType.DMA
    return pl.pallas_call(
        functools.partial(kernel, n),
        out_shape=(out,) * 4,
        in_specs=[vmem] * 4 + [smem] * 2,
        out_specs=(vmem,) * 4,
        scratch_shapes=[
            pltpu.VMEM((HEADS, 2, BLOCK, PACK), jnp.bfloat16),
            pltpu.VMEM((HEADS, SLAB + EXTRA, PACK), jnp.bfloat16),
            pltpu.VMEM((2 * n, BLOCK, PACK), jnp.bfloat16),
            pltpu.VMEM((n, SLAB + EXTRA, PACK), jnp.bfloat16),
            pltpu.VMEM((2 * n, BLOCK, PACK), jnp.float32),
            pltpu.VMEM((n, SLAB, PACK), jnp.bfloat16),
            pltpu.VMEM((HEADS, SLAB, PACK), jnp.bfloat16),
            pltpu.VMEM((n, SLAB, PACK), jnp.bfloat16),
            pltpu.VMEM((HEADS, SLAB, PACK), jnp.bfloat16),
            dma((n,)),
            dma((n,)),
            dma((n,)),
            dma((n,)),
            dma((n,)),
            dma((HEADS,)),
            dma((n,)),
            dma((HEADS,)),
        ],
        compiler_params=pltpu.CompilerParams(
            collective_id=0, has_side_effects=True, vmem_limit_bytes=48 * 1024 * 1024
        ),
    )(queries, keys, values, grad_out, rand_blocks, global_ids)


def solution(mesh):
    rows = P(("dp", "ctx"), None)
    return jax.shard_map(
        functools.partial(local, mesh.shape["ctx"]),
        mesh=mesh,
        in_specs=(rows,) * 5 + (P("dp"),),
        out_specs=(rows,) * 4,
        check_vma=False,
    )
```

time: 289 us -> 70.7 us (0.24)
  the two profiles are of different devices: /device:TPU:8 before, /device:TPU:1 now
where the time goes in v1:
time: 70.7 us; the launch traced here: 69.4 us
  Pallas kernels  60.9 us (86%)
  local copies, waits for them, and re-layouts  7.94 us (11%)
    pallas_call x1, Pallas kernels, local(): pl.pallas_call(functools.partial(kernel, n), out_shape=(out,) * 4, in_spe...  60.9 us
    unnamed x16, local copies, waits for them, and re-layouts  7.94 us

profile of v1, /device:TPU:1, one launch (start us, length us, event | category | flops | bytes accessed | tf_op | source)
XLA Modules:
  0.0 69.4 jit_solution(1914717948772215495)
XLA Ops:
  0.6 0.0 copy-start
  0.6 0.9 %copy-done = bf16[128,1024]{1,0:T(8,128)(2,1)S(1)} copy-done((bf16[128,1024]{1,0:T(8,128)(2,1)S(1)}, bf16[128,1024]{1,0:T(8,128)(2,1)}, u32[]{:S(2)}) %copy-start) | copy-done | bytes 262168
  1.6 0.0 copy-start.1
  1.6 0.9 %copy-done.1 = bf16[128,1024]{1,0:T(8,128)(2,1)S(1)} copy-done((bf16[128,1024]{1,0:T(8,128)(2,1)S(1)}, bf16[128,1024]{1,0:T(8,128)(2,1)}, u32[]{:S(2)}) %copy-start.1) | copy-done | bytes 262168
  2.5 0.0 copy-start.2
  2.5 0.9 %copy-done.2 = bf16[128,1024]{1,0:T(8,128)(2,1)S(1)} copy-done((bf16[128,1024]{1,0:T(8,128)(2,1)S(1)}, bf16[128,1024]{1,0:T(8,128)(2,1)}, u32[]{:S(2)}) %copy-start.2) | copy-done | bytes 262168
  3.5 0.0 copy-start.3
  3.5 0.9 %copy-done.3 = bf16[128,1024]{1,0:T(8,128)(2,1)S(1)} copy-done((bf16[128,1024]{1,0:T(8,128)(2,1)S(1)}, bf16[128,1024]{1,0:T(8,128)(2,1)}, u32[]{:S(2)}) %copy-start.3) | copy-done | bytes 262168
  4.4 0.0 copy-start.4
  4.4 0.7 copy-done.4
  5.1 0.0 copy-start.5
  5.1 0.7 copy-done.5
  5.8 60.9 %shard_map.93 = (bf16[128,1024]{1,0:T(8,128)(2,1)S(1)}, bf16[128,1024]{1,0:T(8,128)(2,1)S(1)}, bf16[128,1024]{1,0:T(8,128)(2,1)S(1)}, bf16[128,1024]{1,0:T(8,128)(2,1)S(1)}) custom-call(bf16[128,1024]{1,0:T(8,128)(2,1)S(1)} %copy-done, bf16[128,1024]{1,0:T(8,128)(2,1)S(1)} %copy-done.1, bf16[128,1024]{1,0:T(8,128)(2,1)S(1)} %copy-done.2, ...), custom_call_target="tpu_custom_call" | custom-call | tf_op jit(solution)/shard_map/pallas_call | solution.py:296
  66.6 0.7 %copy.14 = bf16[128,1024]{1,0:T(8,128)(2,1)} copy(bf16[128,1024]{1,0:T(8,128)(2,1)S(1)} %get-tuple-element.8) | data formatting | bytes 524288
  67.3 0.7 %copy.15 = bf16[128,1024]{1,0:T(8,128)(2,1)} copy(bf16[128,1024]{1,0:T(8,128)(2,1)S(1)} %get-tuple-element.9) | data formatting | bytes 524288
  68.0 0.7 %copy.16 = bf16[128,1024]{1,0:T(8,128)(2,1)} copy(bf16[128,1024]{1,0:T(8,128)(2,1)S(1)} %get-tuple-element.10) | data formatting | bytes 524288
  68.7 0.7 %copy.17 = bf16[128,1024]{1,0:T(8,128)(2,1)} copy(bf16[128,1024]{1,0:T(8,128)(2,1)S(1)} %get-tuple-element.11) | data formatting | bytes 524288
Async XLA Ops:
  0.6 1.0 %copy-start = (bf16[128,1024]{1,0:T(8,128)(2,1)S(1)}, bf16[128,1024]{1,0:T(8,128)(2,1)}, u32[]{:S(2)}) copy-start(bf16[128,1024]{1,0:T(8,128)(2,1)} %q_ref.1) | copy-start | bytes 786436
  1.6 0.9 %copy-start.1 = (bf16[128,1024]{1,0:T(8,128)(2,1)S(1)}, bf16[128,1024]{1,0:T(8,128)(2,1)}, u32[]{:S(2)}) copy-start(bf16[128,1024]{1,0:T(8,128)(2,1)} %k_ref.1) | copy-start | bytes 786436
  2.5 0.9 %copy-start.2 = (bf16[128,1024]{1,0:T(8,128)(2,1)S(1)}, bf16[128,1024]{1,0:T(8,128)(2,1)}, u32[]{:S(2)}) copy-start(bf16[128,1024]{1,0:T(8,128)(2,1)} %v_ref.1) | copy-start | bytes 786436
  3.5 0.9 %copy-start.3 = (bf16[128,1024]{1,0:T(8,128)(2,1)S(1)}, bf16[128,1024]{1,0:T(8,128)(2,1)}, u32[]{:S(2)}) copy-start(bf16[128,1024]{1,0:T(8,128)(2,1)} %g_ref.1) | copy-start | bytes 786436
  4.4 0.7 copy-start.4
  5.1 0.7 copy-start.5

commit v2 on v1

--- a/solution.py
+++ b/solution.py
@@ -20,16 +20,23 @@
 
 def kernel(
     n,
+    q_hbm,
+    k_hbm,
+    v_hbm,
+    g_hbm,
+    rand_hbm,
+    gid_hbm,
+    att_ref,
+    dq_ref,
+    dk_ref,
+    dv_ref,
     q_ref,
     k_ref,
     v_ref,
     g_ref,
     rand_ref,
     gid_ref,
-    att_ref,
-    dq_ref,
-    dk_ref,
-    dv_ref,
+    sem_in,
     a_pack,
     b_pack,
     a_all,
@@ -93,6 +100,20 @@
             device_id_type=pl.DeviceIdType.MESH,
         )
 
+    pairs_in = (
+        (k_hbm, k_ref),
+        (v_hbm, v_ref),
+        (q_hbm, q_ref),
+        (g_hbm, g_ref),
+        (rand_hbm, rand_ref),
+        (gid_hbm, gid_ref),
+    )
+    fetches = [
+        pltpu.make_async_copy(src, dst, sem_in.at[i])
+        for i, (src, dst) in enumerate(pairs_in)
+    ]
+    for fetch in fetches:
+        fetch.start()
     barrier = pltpu.get_barrier_semaphore()
 
     def greet(i, carry):
@@ -106,6 +127,8 @@
 
     lax.fori_loop(1, n, greet, 0)
 
+    fetches[0].wait()
+    fetches[1].wait()
     for pair in range(HEADS // 2):
         cols = slice(PACK * pair, PACK * (pair + 1))
         kt, vt = k_ref[:, cols], v_ref[:, cols]
@@ -121,6 +144,8 @@
 
     lax.fori_loop(1, n, start_a, 0)
 
+    for fetch in fetches[2:]:
+        fetch.wait()
     lane = lax.broadcasted_iota(jnp.int32, (1, SLAB), 1)
     low = lane < BLOCK
     rows = [
@@ -213,38 +238,78 @@
         for r in range(RAND):
             other = partner(c, r)
             places += [2 * other, 2 * other + 1]
+        return places, terms
+
+    def add_terms(places, terms):
         for i, place in enumerate(places):
             acc[place] += terms[i * BLOCK : (i + 1) * BLOCK]
 
+    half_n = n // 2
+    my_pair = me // 2
+
+    def arrive_b(c):
+        @pl.when(c != me)
+        def _():
+            send_b(me, c).wait_recv()
+
     def return_o(c):
-        if share == 1:
+        @pl.when((c != me) & (c % share == my_turn))
+        def _():
             send_o(c, my_head).start()
-        else:
-
-            @pl.when(c % share == my_turn)
-            def _():
-                send_o(c, my_head).start()
-
-    slab(me)
-    o_all[my_head] = o_send[me]
-
-    def step(i, carry):
-        c = (me + n - i) % n
-        send_b(me, c).wait_recv()
-        slab(c)
-        return_o(c)
-        return carry
-
-    lax.fori_loop(1, n, step, 0)
-
-    def return_d(i, carry):
-        c = ((my_head + HEADS - i) % HEADS) * share + my_turn
-        d_send[c] = acc[pl.ds(2 * c, 2)].reshape(SLAB, PACK).astype(jnp.bfloat16)
-        send_d(c, my_head).start()
-        return carry
-
-    lax.fori_loop(1, HEADS, return_d, 0)
-    d_all[my_head] = acc[pl.ds(2 * me, 2)].reshape(SLAB, PACK).astype(jnp.bfloat16)
+
+        @pl.when(c == me)
+        def _():
+            o_all[my_head] = o_send[me]
+
+    def return_d(c):
+        @pl.when((c != me) & (c % share == my_turn))
+        def _():
+            total = acc[pl.ds(2 * c, 2)].reshape(SLAB, PACK)
+            d_send[c] = total.astype(jnp.bfloat16)
+            send_d(c, my_head).start()
+
+        @pl.when(c == me)
+        def _():
+            total = acc[pl.ds(2 * me, 2)].reshape(SLAB, PACK)
+            d_all[my_head] = total.astype(jnp.bfloat16)
+
+    def place_of(j, odd):
+        return 2 * ((my_pair + half_n - j) % half_n) + odd
+
+    def two_slabs(first, second):
+        arrive_b(first)
+        arrive_b(second)
+        done = [slab(first), slab(second)]
+        for places, terms in done:
+            add_terms(places, terms)
+        return_o(first)
+        return_o(second)
+
+    def even_step(t, carry):
+        two_slabs(place_of(2 * t, 0), place_of(2 * t + 1, 0))
+        return carry
+
+    lax.fori_loop(0, half_n // 2, even_step, 0)
+
+    def odd_step(t, carry):
+        first, second = place_of(2 * t, 1), place_of(2 * t + 1, 1)
+        two_slabs(first, second)
+
+        @pl.when(t > 0)
+        def _():
+            return_d((first + 1) % n)
+
+        return_d((second + 1) % n)
+        return carry
+
+    lax.fori_loop(0, half_n // 2, odd_step, 0)
+    return_d((place_of(0, 1) + 1) % n)
+
+    def return_odd(i, carry):
+        return_d(place_of(i, 1))
+        return carry
+
+    lax.fori_loop(0, half_n, return_odd, 0)
 
     def arrive_o(i, carry):
         send_o(me, (my_head + i) % HEADS).wait_recv()
@@ -291,14 +356,20 @@
 def local(n, queries, keys, values, grad_out, rand_blocks, global_ids):
     out = jax.ShapeDtypeStruct(queries.shape, jnp.bfloat16)
     vmem = pl.BlockSpec(memory_space=pltpu.VMEM)
-    smem = pl.BlockSpec(memory_space=pltpu.SMEM)
     dma = pltpu.SemaphoreType.DMA
     return pl.pallas_call(
         functools.partial(kernel, n),
         out_shape=(out,) * 4,
-        in_specs=[vmem] * 4 + [smem] * 2,
+        in_specs=[pl.BlockSpec(memory_space=pltpu.HBM)] * 6,
         out_specs=(vmem,) * 4,
         scratch_shapes=[
+            pltpu.VMEM(queries.shape, jnp.bfloat16),
+            pltpu.VMEM(queries.shape, jnp.bfloat16),
+            pltpu.VMEM(queries.shape, jnp.bfloat16),
+            pltpu.VMEM(queries.shape, jnp.bfloat16),
+            pltpu.SMEM(rand_blocks.shape, jnp.int32),
+            pltpu.SMEM(global_ids.shape, jnp.int32),
+            dma((6,)),
             pltpu.VMEM((HEADS, 2, BLOCK, PACK), jnp.bfloat16),
             pltpu.VMEM((HEADS, SLAB + EXTRA, PACK), jnp.bfloat16),
             pltpu.VMEM((2 * n, BLOCK, PACK), jnp.bfloat16),

time: 70.7 us -> 70.8 us (level); the launches traced: 69.4 us -> 70.5 us
  Pallas kernels: 60.9 us -> 61.9 us
    pallas_call x1, Pallas kernels: 60.9 us -> 61.9 us  [local(): pl.pallas_call(functools.partial(kernel, n), out_shape=(out,) * 4, in_spe...]
where the time goes in v2:
time: 70.8 us; the launch traced here: 70.5 us
  Pallas kernels  61.9 us (87%)
  local copies, waits for them, and re-layouts  7.94 us (11%)
    pallas_call x1, Pallas kernels, local(): pl.pallas_call(functools.partial(kernel, n), out_shape=(out,) * 4, in_spe...  61.9 us
    unnamed x16, local copies, waits for them, and re-layouts  7.94 us

profile of v2, /device:TPU:1, one launch (start us, length us, event | category | flops | bytes accessed | tf_op | source)
XLA Modules:
  0.0 70.5 jit_solution(14157506553736328793)
XLA Ops:
  0.6 0.0 copy-start
  0.6 0.9 %copy-done = bf16[128,1024]{1,0:T(8,128)(2,1)S(1)} copy-done((bf16[128,1024]{1,0:T(8,128)(2,1)S(1)}, bf16[128,1024]{1,0:T(8,128)(2,1)}, u32[]{:S(2)}) %copy-start) | copy-done | bytes 262168
  1.6 0.0 copy-start.1
  1.6 0.9 %copy-done.1 = bf16[128,1024]{1,0:T(8,128)(2,1)S(1)} copy-done((bf16[128,1024]{1,0:T(8,128)(2,1)S(1)}, bf16[128,1024]{1,0:T(8,128)(2,1)}, u32[]{:S(2)}) %copy-start.1) | copy-done | bytes 262168
  2.5 0.0 copy-start.2
  2.5 0.9 %copy-done.2 = bf16[128,1024]{1,0:T(8,128)(2,1)S(1)} copy-done((bf16[128,1024]{1,0:T(8,128)(2,1)S(1)}, bf16[128,1024]{1,0:T(8,128)(2,1)}, u32[]{:S(2)}) %copy-start.2) | copy-done | bytes 262168
  3.5 0.0 copy-start.3
  3.5 0.9 %copy-done.3 = bf16[128,1024]{1,0:T(8,128)(2,1)S(1)} copy-done((bf16[128,1024]{1,0:T(8,128)(2,1)S(1)}, bf16[128,1024]{1,0:T(8,128)(2,1)}, u32[]{:S(2)}) %copy-start.3) | copy-done | bytes 262168
  4.4 0.0 copy-start.4
  4.4 0.7 copy-done.4
  5.1 0.0 copy-start.5
  5.1 0.7 copy-done.5
  5.8 61.9 %shard_map.93 = (bf16[128,1024]{1,0:T(8,128)(2,1)S(1)}, bf16[128,1024]{1,0:T(8,128)(2,1)S(1)}, bf16[128,1024]{1,0:T(8,128)(2,1)S(1)}, bf16[128,1024]{1,0:T(8,128)(2,1)S(1)}) custom-call(bf16[128,1024]{1,0:T(8,128)(2,1)S(1)} %copy-done, bf16[128,1024]{1,0:T(8,128)(2,1)S(1)} %copy-done.1, bf16[128,1024]{1,0:T(8,128)(2,1)S(1)} %copy-done.2, ...), custom_call_target="tpu_custom_call" | custom-call | tf_op jit(solution)/shard_map/pallas_call | solution.py:360
  67.7 0.7 copy.14
  68.4 0.7 copy.15
  69.1 0.7 copy.16
  69.8 0.7 copy.17
Async XLA Ops:
  0.6 1.0 %copy-start = (bf16[128,1024]{1,0:T(8,128)(2,1)S(1)}, bf16[128,1024]{1,0:T(8,128)(2,1)}, u32[]{:S(2)}) copy-start(bf16[128,1024]{1,0:T(8,128)(2,1)} %q_hbm.1) | copy-start | bytes 786436
  1.6 0.9 %copy-start.1 = (bf16[128,1024]{1,0:T(8,128)(2,1)S(1)}, bf16[128,1024]{1,0:T(8,128)(2,1)}, u32[]{:S(2)}) copy-start(bf16[128,1024]{1,0:T(8,128)(2,1)} %k_hbm.1) | copy-start | bytes 786436
  2.5 0.9 %copy-start.2 = (bf16[128,1024]{1,0:T(8,128)(2,1)S(1)}, bf16[128,1024]{1,0:T(8,128)(2,1)}, u32[]{:S(2)}) copy-start(bf16[128,1024]{1,0:T(8,128)(2,1)} %v_hbm.1) | copy-start | bytes 786436
  3.5 0.9 %copy-start.3 = (bf16[128,1024]{1,0:T(8,128)(2,1)S(1)}, bf16[128,1024]{1,0:T(8,128)(2,1)}, u32[]{:S(2)}) copy-start(bf16[128,1024]{1,0:T(8,128)(2,1)} %g_hbm.1) | copy-start | bytes 786436
  4.4 0.7 copy-start.4
  5.1 0.7 copy-start.5

commit v3 on v2

--- a/solution.py
+++ b/solution.py
@@ -14,7 +14,6 @@
 GLOBALS = 2
 SLAB = 2 * BLOCK
 PACK = 2 * HEAD_DIM
-EXTRA = 16
 SCORE_FLOOR = -1e30
 
 
@@ -46,6 +45,10 @@
     o_all,
     d_send,
     d_all,
+    c_pack,
+    c_all,
+    sem_cs,
+    sem_cr,
     sem_as,
     sem_ar,
     sem_bs,
@@ -79,6 +82,36 @@
             device_id={"ctx": dest},
             device_id_type=pl.DeviceIdType.MESH,
         )
+
+    def send_c(dest, origin):
+        return pltpu.make_async_remote_copy(
+            src_ref=c_pack,
+            dst_ref=c_all.at[origin],
+            send_sem=sem_cs.at[dest],
+            recv_sem=sem_cr.at[origin],
+            device_id={"ctx": dest},
+            device_id_type=pl.DeviceIdType.MESH,
+        )
+
+    half_n = n // 2
+    side = me // half_n
+    spot = me % half_n
+
+    def far(t):
+        return (1 - side) * half_n + (spot + t) % half_n
+
+    def near(t):
+        return side * half_n + (spot + t) % half_n
+
+    def to_all(send):
+        send(far(0), me).start()
+
+        def body(t, carry):
+            send(far(t), me).start()
+            send(near(t), me).start()
+            return carry
+
+        lax.fori_loop(1, half_n, body, 0)
 
     def send_o(dest, head):
         return pltpu.make_async_remote_copy(
@@ -138,44 +171,36 @@
             a_pack[2 * pair + odd] = both.reshape(2, BLOCK, PACK)
     pl.semaphore_wait(barrier, n - 1)
 
-    def start_a(i, carry):
-        send_a((me + i) % n, me).start()
-        return carry
-
-    lax.fori_loop(1, n, start_a, 0)
+    to_all(send_a)
 
     for fetch in fetches[2:]:
         fetch.wait()
     lane = lax.broadcasted_iota(jnp.int32, (1, SLAB), 1)
     low = lane < BLOCK
-    rows = [
-        jnp.where(low, rand_ref[0, r], rand_ref[1, r]).astype(jnp.float32)
-        for r in range(RAND)
-    ]
-    rows.append(jnp.zeros((EXTRA - RAND, SLAB), jnp.float32))
-    picks = jnp.concatenate(rows, axis=0).astype(jnp.bfloat16)
+    code = jnp.where(low, rand_ref[0, 0], rand_ref[1, 0])
+    for r in range(1, RAND):
+        code += jnp.where(low, rand_ref[0, r], rand_ref[1, r]) * 2**r
+    c_pack[...] = code.astype(jnp.float32)
     for pair in range(HEADS // 2):
         cols = slice(PACK * pair, PACK * (pair + 1))
         qt, gt = q_ref[:, cols], g_ref[:, cols]
         for odd in range(2):
             half = slice(HEAD_DIM * odd, HEAD_DIM * (odd + 1))
-            b_pack[2 * pair + odd, :SLAB] = jnp.concatenate(
+            b_pack[2 * pair + odd] = jnp.concatenate(
                 [qt[:, half], gt[:, half]], axis=1
             )
-            b_pack[2 * pair + odd, SLAB:] = picks
-
-    def start_b(i, carry):
-        send_b((me + i) % n, me).start()
-        return carry
-
-    lax.fori_loop(1, n, start_b, 0)
+
+    to_all(send_c)
+    to_all(send_b)
 
     a_all[pl.ds(2 * me, 2)] = a_pack[my_head]
     b_all[me] = b_pack[my_head]
+    c_all[me] = c_pack[...]
     acc[...] = jnp.zeros_like(acc)
 
     def arrive_a(i, carry):
         send_a(me, (me + n - i) % n).wait_recv()
+        send_c(me, (me + n - i) % n).wait_recv()
         return carry
 
     lax.fori_loop(1, n, arrive_a, 0)
@@ -190,8 +215,7 @@
         return c + d - 2 * d * ((c // d) % 2)
 
     def slab(c):
-        mixed = b_all[c]
-        tokens = mixed[:SLAB]
+        tokens = b_all[c]
         both = jnp.concatenate([tokens * keep_q, tokens * keep_g], axis=0)
         before = jnp.maximum(2 * c - 1, 0)
         after = jnp.minimum(2 * c + 2, 2 * n - 1)
@@ -206,16 +230,16 @@
         )
         scores = prod[:, :SLAB]
         grads = prod[:, SLAB:]
-        chosen = mixed[SLAB:].astype(jnp.float32)
+        code = c_all[c].astype(jnp.int32)
         segs = [scores[i * BLOCK : (i + 1) * BLOCK] for i in range(len(listed))]
         left_ok = lane + jnp.where(c > 0, 0, SLAB) < BLOCK
         right_ok = lane - jnp.where(c < n - 1, 0, SLAB) >= BLOCK
         segs[0] = jnp.where(left_ok, segs[0], SCORE_FLOOR)
         segs[3] = jnp.where(right_ok, segs[3], SCORE_FLOOR)
         for r in range(RAND):
-            pick = chosen[r : r + 1]
-            segs[4 + 2 * r] = jnp.where(pick < 0.5, segs[4 + 2 * r], SCORE_FLOOR)
-            segs[5 + 2 * r] = jnp.where(pick > 0.5, segs[5 + 2 * r], SCORE_FLOOR)
+            pick = (code >> r) & 1
+            segs[4 + 2 * r] = jnp.where(pick == 0, segs[4 + 2 * r], SCORE_FLOOR)
+            segs[5 + 2 * r] = jnp.where(pick == 1, segs[5 + 2 * r], SCORE_FLOOR)
         scores = jnp.concatenate(segs + [scores[own_rows:]], axis=0)
         highest = jnp.max(scores, axis=0, keepdims=True)
         raw = jnp.exp(scores - highest)
@@ -244,9 +268,6 @@
         for i, place in enumerate(places):
             acc[place] += terms[i * BLOCK : (i + 1) * BLOCK]
 
-    half_n = n // 2
-    my_pair = me // 2
-
     def arrive_b(c):
         @pl.when(c != me)
         def _():
@@ -273,8 +294,10 @@
             total = acc[pl.ds(2 * me, 2)].reshape(SLAB, PACK)
             d_all[my_head] = total.astype(jnp.bfloat16)
 
+    steps = half_n // 2
+
     def place_of(j, odd):
-        return 2 * ((my_pair + half_n - j) % half_n) + odd
+        return 2 * ((spot // 2 + steps - j) % steps) + odd
 
     def two_slabs(first, second):
         arrive_b(first)
@@ -285,31 +308,35 @@
         return_o(first)
         return_o(second)
 
+    def both_sides(act, place):
+        act((1 - side) * half_n + place)
+        act(side * half_n + place)
+
     def even_step(t, carry):
-        two_slabs(place_of(2 * t, 0), place_of(2 * t + 1, 0))
-        return carry
-
-    lax.fori_loop(0, half_n // 2, even_step, 0)
+        place = place_of(t, 0)
+        two_slabs((1 - side) * half_n + place, side * half_n + place)
+        return carry
+
+    lax.fori_loop(0, steps, even_step, 0)
 
     def odd_step(t, carry):
-        first, second = place_of(2 * t, 1), place_of(2 * t + 1, 1)
-        two_slabs(first, second)
+        place = place_of(t, 1)
+        two_slabs((1 - side) * half_n + place, side * half_n + place)
 
         @pl.when(t > 0)
         def _():
-            return_d((first + 1) % n)
-
-        return_d((second + 1) % n)
-        return carry
-
-    lax.fori_loop(0, half_n // 2, odd_step, 0)
-    return_d((place_of(0, 1) + 1) % n)
-
-    def return_odd(i, carry):
-        return_d(place_of(i, 1))
-        return carry
-
-    lax.fori_loop(0, half_n, return_odd, 0)
+            both_sides(return_d, (place + 1) % half_n)
+
+        return carry
+
+    lax.fori_loop(0, steps, odd_step, 0)
+    both_sides(return_d, (place_of(0, 1) + 1) % half_n)
+
+    def return_odd(t, carry):
+        both_sides(return_d, place_of(t, 1))
+        return carry
+
+    lax.fori_loop(0, steps, return_odd, 0)
 
     def arrive_o(i, carry):
         send_o(me, (my_head + i) % HEADS).wait_recv()
@@ -340,6 +367,7 @@
     def sent_in(i, carry):
         send_a((me + i) % n, me).wait_send()
         send_b((me + i) % n, me).wait_send()
+        send_c((me + i) % n, me).wait_send()
         return carry
 
     lax.fori_loop(1, n, sent_in, 0)
@@ -360,7 +388,7 @@
     return pl.pallas_call(
         functools.partial(kernel, n),
         out_shape=(out,) * 4,
-        in_specs=[pl.BlockSpec(memory_space=pltpu.HBM)] * 6,
+        in_specs=[pl.BlockSpec(memory_space=pl.ANY)] * 6,
         out_specs=(vmem,) * 4,
         scratch_shapes=[
             pltpu.VMEM(queries.shape, jnp.bfloat16),
@@ -371,14 +399,18 @@
             pltpu.SMEM(global_ids.shape, jnp.int32),
             dma((6,)),
             pltpu.VMEM((HEADS, 2, BLOCK, PACK), jnp.bfloat16),
-            pltpu.VMEM((HEADS, SLAB + EXTRA, PACK), jnp.bfloat16),
+            pltpu.VMEM((HEADS, SLAB, PACK), jnp.bfloat16),
             pltpu.VMEM((2 * n, BLOCK, PACK), jnp.bfloat16),
-            pltpu.VMEM((n, SLAB + EXTRA, PACK), jnp.bfloat16),
+            pltpu.VMEM((n, SLAB, PACK), jnp.bfloat16),
             pltpu.VMEM((2 * n, BLOCK, PACK), jnp.float32),
             pltpu.VMEM((n, SLAB, PACK), jnp.bfloat16),
             pltpu.VMEM((HEADS, SLAB, PACK), jnp.bfloat16),
             pltpu.VMEM((n, SLAB, PACK), jnp.bfloat16),
             pltpu.VMEM((HEADS, SLAB, PACK), jnp.bfloat16),
+            pltpu.VMEM((1, PACK), jnp.float32),
+            pltpu.VMEM((n, 1, PACK), jnp.float32),
+            dma((n,)),
+            dma((n,)),
             dma((n,)),
             dma((n,)),
             dma((n,)),
@@ -389,7 +421,7 @@
             dma((HEADS,)),
         ],
         compiler_params=pltpu.CompilerParams(
-            collective_id=0, has_side_effects=True, vmem_limit_bytes=48 * 1024 * 1024
+            collective_id=0, has_side_effects=True, vmem_limit_bytes=63 * 1024 * 1024
         ),
     )(queries, keys, values, grad_out, rand_blocks, global_ids)
 

time: 70.8 us -> 61.2 us (0.86)
  Pallas kernels: 61.9 us -> 55.8 us
  local copies, waits for them, and re-layouts: 7.94 us -> 4.5 us
    pallas_call x1, Pallas kernels: 61.9 us -> 55.8 us  [local(): pl.pallas_call(functools.partial(kernel, n), out_shape=(out,) * 4, in_spe...]
    unnamed x16 -> x10, local copies, waits for them, and re-layouts: 7.94 us -> 4.5 us
where the time goes in v3:
time: 61.2 us; the launch traced here: 61 us
  Pallas kernels  55.8 us (91%)
  local copies, waits for them, and re-layouts  4.5 us (7%)
  between operations  0.65 us (1%)
    pallas_call x1, Pallas kernels, local(): pl.pallas_call(functools.partial(kernel, n), out_shape=(out,) * 4, in_spe...  55.8 us
    unnamed x10, local copies, waits for them, and re-layouts  4.5 us

profile of v3, /device:TPU:1, one launch (start us, length us, event | category | flops | bytes accessed | tf_op | source)
XLA Modules:
  0.0 61.0 jit_solution(659839491573483229)
XLA Ops:
  0.6 55.8 %shard_map.93 = (bf16[128,1024]{1,0:T(8,128)(2,1)}, bf16[128,1024]{1,0:T(8,128)(2,1)}, bf16[128,1024]{1,0:T(8,128)(2,1)}, bf16[128,1024]{1,0:T(8,128)(2,1)}) custom-call(bf16[128,1024]{1,0:T(8,128)(2,1)} %q_hbm.1, bf16[128,1024]{1,0:T(8,128)(2,1)} %k_hbm.1, bf16[128,1024]{1,0:T(8,128)(2,1)} %v_hbm.1, bf16[128,1024]{1,0:T(8,128)(2,1)} %g_hbm.1, ...), custom_call_target="tpu_custom_call" | custom-call | tf_op jit(solution)/shard_map/pallas_call | solution.py:388
  56.5 0.0 copy-start.2
  56.5 1.7 %copy.14 = bf16[128,1024]{1,0:T(8,128)(2,1)} copy(bf16[128,1024]{1,0:T(8,128)(2,1)} %get-tuple-element.8) | data formatting | bytes 524288
  58.2 0.0 copy-done.2
  58.2 0.0 copy-start.1
  58.2 0.7 %copy.15 = bf16[128,1024]{1,0:T(8,128)(2,1)} copy(bf16[128,1024]{1,0:T(8,128)(2,1)S(1)} %copy-done.2) | data formatting | bytes 524288
  58.9 0.3 copy-done.1
  59.2 0.0 copy-start
  59.2 0.7 %copy.16 = bf16[128,1024]{1,0:T(8,128)(2,1)} copy(bf16[128,1024]{1,0:T(8,128)(2,1)S(1)} %copy-done.1) | data formatting | bytes 524288
  59.9 0.3 copy-done
  60.3 0.7 %copy.17 = bf16[128,1024]{1,0:T(8,128)(2,1)} copy(bf16[128,1024]{1,0:T(8,128)(2,1)S(1)} %copy-done) | data formatting | bytes 524288
Async XLA Ops:
  56.5 1.7 %copy-start.2 = (bf16[128,1024]{1,0:T(8,128)(2,1)S(1)}, bf16[128,1024]{1,0:T(8,128)(2,1)}, u32[]{:S(2)}) copy-start(bf16[128,1024]{1,0:T(8,128)(2,1)} %get-tuple-element.9) | copy-start | bytes 786436
  58.2 1.0 %copy-start.1 = (bf16[128,1024]{1,0:T(8,128)(2,1)S(1)}, bf16[128,1024]{1,0:T(8,128)(2,1)}, u32[]{:S(2)}) copy-start(bf16[128,1024]{1,0:T(8,128)(2,1)} %get-tuple-element.10) | copy-start | bytes 786436
  59.2 1.0 %copy-start = (bf16[128,1024]{1,0:T(8,128)(2,1)S(1)}, bf16[128,1024]{1,0:T(8,128)(2,1)}, u32[]{:S(2)}) copy-start(bf16[128,1024]{1,0:T(8,128)(2,1)} %get-tuple-element.11) | copy-start | bytes 786436
